TPU v7x, 128 devices: a whole 4x4x4 slice. The times are simulated.
128 devices in a mesh: band: 16 (over z, x), pw: 8 (over y, core).
Axes of the slice: x: 4, y: 4, z: 4, core: 2. Of those that a mesh axis runs over, the one named last changes fastest.
Arguments:
- columns: bfloat16 [256, 8192, 256], P('band', 'pw'), may hold values from -2000 to 2000
- counts: int32 [8], replicated, may hold values from 1 to 1024, 6144 in all
Outputs:
- orthonormal: bfloat16 [256, 8192, 256], P('band', 'pw')
Inputs may be any that keep to these rules, and one draw needn't show every extreme that they name: The counts add up to 6144, and the largest is exactly 1024.
All inputs are finite; a program needn't handle non-finite values.
Results may differ from a plain program's by a relative error of at most 0.0069.
Values may be sent and summed in bfloat16 or wider, within the bound.
No kernel may reach another device: no remote copies, remote signals or barrier semaphores. Data moves between devices by JAX's collectives and lax.ppermute only.
A program may use at most 128 MiB of HBM per device.

v0:
```python
import functools

import jax
import jax.numpy as jnp
import numpy as np
from jax import lax
from jax.experimental import pallas as pl
from jax.experimental.pallas import tpu as pltpu
from jax.sharding import PartitionSpec as P

ITERS = 8
GROUP = 16
MIB = 1024 * 1024


def hartley(stick_length):
    rows = np.arange(stick_length, dtype=np.int32)
    phase = (rows[:, None] * rows[None, :] % stick_length).astype(np.float32)
    angle = phase * np.float32(2.0 * np.pi / stick_length)
    table = (np.cos(angle) + np.sin(angle)) / np.sqrt(np.float32(stick_length))
    return jnp.asarray(table.astype(jnp.bfloat16))


def dot(left, right):
    return jnp.dot(left, right, preferred_element_type=jnp.float32)


def params(mib):
    return pltpu.CompilerParams(vmem_limit_bytes=mib * MIB)


def transform_kernel(counts_ref, table_ref, columns_ref, out_ref, buf, table, sems, table_sem):
    members, each, bands, length = out_ref.shape

    def fetch(i):
        rows = pl.ds(pl.multiple_of(i * each, each), each)
        return pltpu.make_async_copy(columns_ref.at[:, rows, :], buf.at[i], sems.at[i])

    table_copy = pltpu.make_async_copy(table_ref, table, table_sem)
    table_copy.start()
    for i in range(members):
        fetch(i).start()
    limit = counts_ref[lax.axis_index("pw")]
    row_slot = lax.broadcasted_iota(jnp.int32, (each * bands, length), 0) // bands
    table_copy.wait()

    def step(i, carry):
        fetch(i).wait()
        turned = [
            jnp.swapaxes(buf[i, :, s : s + GROUP, :], 0, 1).reshape(GROUP * bands, length)
            for s in range(0, each, GROUP)
        ]
        value = dot(jnp.concatenate(turned, axis=0), table[...])
        value = jnp.where(row_slot < limit - i * each, value, 0.0).astype(jnp.bfloat16)
        out_ref[i] = value.reshape(each, bands, length)
        return carry

    lax.fori_loop(0, members, step, 0)


def transform(columns, counts, members):
    bands, slots, length = columns.shape
    each = slots // members
    return pl.pallas_call(
        transform_kernel,
        in_specs=[
            pl.BlockSpec(memory_space=pltpu.SMEM),
            pl.BlockSpec(memory_space=pltpu.HBM),
            pl.BlockSpec(memory_space=pltpu.HBM),
        ],
        out_specs=pl.BlockSpec(memory_space=pltpu.VMEM),
        out_shape=jax.ShapeDtypeStruct((members, each, bands, length), jnp.bfloat16),
        scratch_shapes=[
            pltpu.VMEM((members, bands, each, length), jnp.bfloat16),
            pltpu.VMEM((length, length), jnp.bfloat16),
            pltpu.SemaphoreType.DMA((members,)),
            pltpu.SemaphoreType.DMA,
        ],
        compiler_params=params(44),
        name="transform",
    )(counts, hartley(length), columns)


def fetch_slots(sticks_ref, buf, sems, i, each):
    rows = pl.ds(i * each, each)
    return pltpu.make_async_copy(sticks_ref.at[:, rows], buf.at[:, rows], sems.at[i])


def gram_kernel(each, sticks_ref, out_ref, buf, sems):
    members, slots, bands, length = sticks_ref.shape
    total = members * bands
    steps = slots // each
    for i in range(steps):
        fetch_slots(sticks_ref, buf, sems, i, each).start()
    acc = jnp.zeros((total, total), jnp.float32)
    for i in range(steps):
        fetch_slots(sticks_ref, buf, sems, i, each).wait()
        rows = [buf[:, i * each + s].reshape(total, length) for s in range(each)]
        wide = jnp.concatenate(rows, axis=1)
        acc += lax.dot_general(
            wide, wide, (((1,), (1,)), ((), ())), preferred_element_type=jnp.float32
        )
    piece = 0
    for r in range(0, total, 8):
        for c in range(0, total, 128):
            for half in range(2):
                out_ref[piece] = acc[r + 4 * half : r + 4 * half + 4, c : c + 128]
                piece += 1


def gram(sticks, each):
    members, slots, bands, length = sticks.shape
    total = members * bands
    return pl.pallas_call(
        functools.partial(gram_kernel, each),
        in_specs=[pl.BlockSpec(memory_space=pltpu.HBM)],
        out_specs=pl.BlockSpec(memory_space=pltpu.VMEM),
        out_shape=jax.ShapeDtypeStruct((total * total // 512, 4, 128), jnp.float32),
        scratch_shapes=[
            pltpu.VMEM(sticks.shape, jnp.bfloat16),
            pltpu.SemaphoreType.DMA((slots // each,)),
        ],
        compiler_params=params(52),
        name="gram",
    )(sticks)


def split(value):
    high = value.astype(jnp.bfloat16)
    return high, (value - high.astype(jnp.float32)).astype(jnp.bfloat16)


def product(left, right):
    left_high, left_low = left
    right_high, right_low = right
    return dot(left_high, right_high) + (dot(left_high, right_low) + dot(left_low, right_high))


def rotate_kernel(each, counts_ref, sums_ref, sticks_ref, out_ref, buf, sems, turn_ref):
    members, slots, bands, length = sticks_ref.shape
    size = members * bands
    steps = slots // each
    for i in range(steps):
        fetch_slots(sticks_ref, buf, sems, i, each).start()

    live = counts_ref[0]
    for i in range(1, counts_ref.shape[0]):
        live += counts_ref[i]
    tiles = size // 128
    pieces = [sums_ref[i] for i in range(sums_ref.shape[0])]
    whole = [jnp.concatenate(pieces[i : i + 2], axis=0) for i in range(0, len(pieces), 2)]
    lines = [jnp.concatenate(whole[i : i + tiles], axis=1) for i in range(0, len(whole), tiles)]
    correlation = jnp.concatenate(lines, axis=0) / (live.astype(jnp.float32) * length)
    row = lax.broadcasted_iota(jnp.int32, (size, size), 0)
    col = lax.broadcasted_iota(jnp.int32, (size, size), 1)
    ident = jnp.where(row == col, 1.0, 0.0)
    scale = jnp.sum(correlation * ident, keepdims=True) / size
    y_iter = correlation / scale

    z_iter = 1.5 * ident - 0.5 * y_iter
    z_split = split(z_iter)
    y_split = split(product(split(y_iter), z_split))
    for step in range(1, ITERS):
        p_split = split(1.5 * ident - 0.5 * product(z_split, y_split))
        if step < ITERS - 1:
            y_split = split(product(y_split, p_split))
        z_iter = product(p_split, z_split)
        z_split = split(z_iter)
    turn_ref[...] = (z_iter / jnp.sqrt(scale)).T.astype(jnp.bfloat16)

    turn = turn_ref[...]
    for i in range(steps):
        fetch_slots(sticks_ref, buf, sems, i, each).wait()
    for i in range(steps):
        for s in range(i * each, (i + 1) * each):
            value = dot(turn, buf[:, s].reshape(size, length)).astype(jnp.bfloat16)
            out_ref[:, s] = value.reshape(members, bands, length)


def rotate(counts, sums, sticks, each):
    members, slots, bands, length = sticks.shape
    size = members * bands
    return pl.pallas_call(
        functools.partial(rotate_kernel, each),
        in_specs=[
            pl.BlockSpec(memory_space=pltpu.SMEM),
            pl.BlockSpec(memory_space=pltpu.VMEM),
            pl.BlockSpec(memory_space=pltpu.HBM),
        ],
        out_specs=pl.BlockSpec(memory_space=pltpu.VMEM),
        out_shape=jax.ShapeDtypeStruct(sticks.shape, jnp.bfloat16),
        scratch_shapes=[
            pltpu.VMEM(sticks.shape, jnp.bfloat16),
            pltpu.SemaphoreType.DMA((slots // each,)),
            pltpu.VMEM((size, size), jnp.bfloat16),
        ],
        compiler_params=params(44),
        name="rotate",
    )(counts, sums, sticks)


def place_kernel(in_ref, out_ref, buf, sems):
    members, each, bands, length = in_ref.shape

    def store(i):
        rows = pl.ds(pl.multiple_of(i * each, each), each)
        return pltpu.make_async_copy(buf.at[i], out_ref.at[:, rows, :], sems.at[i])

    def step(i, carry):
        for s in range(0, each, GROUP):
            buf[i, :, s : s + GROUP, :] = jnp.swapaxes(in_ref[i, s : s + GROUP], 0, 1)
        store(i).start()
        return carry

    def finish(i, carry):
        store(i).wait()
        return carry

    lax.fori_loop(0, members, step, 0)
    lax.fori_loop(0, members, finish, 0)


def place(rotated):
    members, each, bands, length = rotated.shape
    return pl.pallas_call(
        place_kernel,
        in_specs=[pl.BlockSpec(memory_space=pltpu.VMEM)],
        out_specs=pl.BlockSpec(memory_space=pltpu.HBM),
        out_shape=jax.ShapeDtypeStruct((bands, members * each, length), jnp.bfloat16),
        scratch_shapes=[
            pltpu.VMEM((members, bands, each, length), jnp.bfloat16),
            pltpu.SemaphoreType.DMA((members,)),
        ],
        compiler_params=params(32),
        name="place",
    )(rotated)


def whole_sum(shares, axes):
    share = lax.all_to_all(shares, axes, 0, 0, tiled=True).sum(0)
    spread = jnp.broadcast_to(share[None], shares.shape)
    return lax.all_to_all(spread, axes, 0, 0, tiled=True)


def make_local(members):
    def local(columns, counts):
        send = transform(columns, counts, members)
        sticks = lax.all_to_all(send, "band", 0, 0, tiled=True)
        sums = whole_sum(gram(sticks, 8), ("band", "pw"))
        rotated = rotate(counts, sums, sticks, 16)
        return place(lax.all_to_all(rotated, "band", 0, 0, tiled=True))

    return local


def solution(mesh):
    return jax.shard_map(
        make_local(mesh.shape["band"]),
        mesh=mesh,
        in_specs=(P("band", "pw", None), P()),
        out_specs=P("band", "pw", None),
        check_vma=False,
    )
```

profile of v0, /device:TPU:0, one launch (start us, length us, event | category | flops | bytes accessed | tf_op | source)
XLA Modules:
  0.0 261.5 jit_solution(17359223362082610677)
XLA Ops:
  0.0 0.0 copy-start
  0.0 0.9 copy-done
  0.9 0.0 copy-start.1
  0.9 0.7 copy-done.1
  1.6 7.0 %transform.1 = bf16[16,64,16,256]{3,2,1,0:T(8,128)(2,1)S(1)} custom-call(s32[8]{0:T(128)S(1)} %copy-done.1, bf16[256,256]{1,0:T(8,128)(2,1)S(1)} %copy-done, bf16[16,1024,256]{2,1,0:T(8,128)(2,1)} %columns_ref.1), custom_call_target="tpu_custom_call" | custom-call | tf_op jit(solution)/shard_map/transform/pallas_call | solution.py:64
  8.5 103.7 %all_to_all.20.sticks_ref = bf16[16,64,16,256]{3,2,1,0:T(8,128)(2,1)} all-to-all(bf16[16,64,16,256]{3,2,1,0:T(8,128)(2,1)S(1)} %transform.1), channel_id=1, replica_groups=mesh['band'=16,'pw'=8] {'band'}, dimensions={0} | all-to-all | bytes 16777216 | tf_op jit(solution)/shard_map/all_to_all | solution.py:248
  112.2 0.0 copy-start.2
  112.2 6.6 %gram.1 = f32[128,4,128]{2,1,0:T(4,128)S(1)} custom-call(bf16[16,64,16,256]{3,2,1,0:T(8,128)(2,1)} %all_to_all.20.sticks_ref), custom_call_target="tpu_custom_call" | custom-call | tf_op jit(solution)/shard_map/gram/pallas_call | solution.py:114
  118.9 16.9 %all_to_all.21 = f32[128,4,128]{2,1,0:T(4,128)S(1)} all-to-all(f32[128,4,128]{2,1,0:T(4,128)S(1)} %gram.1), channel_id=1, replica_groups=mesh['band'=16,'pw'=8] {'band','pw'}, dimensions={0} | all-to-all | bytes 524288 | tf_op jit(solution)/shard_map/all_to_all | solution.py:240
  135.7 0.1 reduce_sum.9
  135.9 15.2 %all_to_all.22.sums_ref = f32[128,4,128]{2,1,0:T(4,128)S(1)} all-to-all(f32[128,4,128]{2,1,0:T(4,128)S(1)} %broadcast_in_dim.2), channel_id=1, replica_groups=mesh['band'=16,'pw'=8] {'band','pw'}, dimensions={0} | all-to-all | bytes 524288 | tf_op jit(solution)/shard_map/all_to_all | solution.py:242
  151.1 0.0 copy-done.2
  151.1 8.1 %rotate.1 = bf16[16,64,16,256]{3,2,1,0:T(8,128)(2,1)S(1)} custom-call(s32[8]{0:T(128)S(1)} %copy-done.2, f32[128,4,128]{2,1,0:T(4,128)S(1)} %all_to_all.22.sums_ref, bf16[16,64,16,256]{3,2,1,0:T(8,128)(2,1)} %all_to_all.20.sticks_ref), custom_call_target="tpu_custom_call" | custom-call | tf_op jit(solution)/shard_map/rotate/pallas_call | solution.py:183
  159.2 98.7 %all_to_all.23.in_ref = bf16[16,64,16,256]{3,2,1,0:T(8,128)(2,1)S(1)} all-to-all(bf16[16,64,16,256]{3,2,1,0:T(8,128)(2,1)S(1)} %rotate.1), channel_id=1, replica_groups=mesh['band'=16,'pw'=8] {'band'}, dimensions={0} | all-to-all | bytes 16777216 | tf_op jit(solution)/shard_map/all_to_all | solution.py:251
  258.0 3.5 %place.1 = bf16[16,1024,256]{2,1,0:T(8,128)(2,1)} custom-call(bf16[16,64,16,256]{3,2,1,0:T(8,128)(2,1)S(1)} %all_to_all.23.in_ref), custom_call_target="tpu_custom_call" | custom-call | tf_op jit(solution)/shard_map/place/pallas_call | solution.py:225
  (1 shorter events, 0.0 us)
Async XLA Ops:
  0.0 0.9 copy-start
  0.9 0.7 copy-start.1
  112.2 38.9 %copy-start.2 = (s32[8]{0:T(128)S(1)}, s32[8]{0:T(128)}, u32[]{:S(2)}) copy-start(s32[8]{0:T(128)} %counts_ref.3) | copy-start | bytes 100
where the time goes:
time: 262 us
  blocking collectives  234 us (89%)
  Pallas kernels  25.3 us (10%)
    all_to_all x1, blocking collectives, local(): sticks = lax.all_to_all(send, 'band', 0, 0, tiled=True)  104 us
    all_to_all x1, blocking collectives, local(): return place(lax.all_to_all(rotated, 'band', 0, 0, tiled=True))  98.7 us
    all_to_all x1, blocking collectives, whole_sum(): share = lax.all_to_all(shares, axes, 0, 0, tiled=True).sum(0)  16.9 us
    all_to_all x1, blocking collectives, whole_sum(): return lax.all_to_all(spread, axes, 0, 0, tiled=True)  15.2 us
    pallas_call x1, Pallas kernels, rotate(): pl.pallas_call(functools.partial(rotate_kernel, each), in_specs=[pl.Block...  8.1 us
    pallas_call x1, Pallas kernels, transform(): pl.pallas_call(transform_kernel, in_specs=[pl.BlockSpec(memory_space=pltp...  6.98 us
    pallas_call x1, Pallas kernels, gram(): pl.pallas_call(functools.partial(gram_kernel, each), in_specs=[pl.BlockSp...  6.64 us

commit v1 on v0

--- a/solution.py
+++ b/solution.py
@@ -31,36 +31,43 @@
 
 def transform_kernel(counts_ref, table_ref, columns_ref, out_ref, buf, table, sems, table_sem):
     members, each, bands, length = out_ref.shape
+    steps = buf.shape[0]
+    span = buf.shape[2]
+    per_member = each // GROUP
 
     def fetch(i):
-        rows = pl.ds(pl.multiple_of(i * each, each), each)
+        rows = pl.ds(pl.multiple_of(i * span, span), span)
         return pltpu.make_async_copy(columns_ref.at[:, rows, :], buf.at[i], sems.at[i])
 
     table_copy = pltpu.make_async_copy(table_ref, table, table_sem)
     table_copy.start()
-    for i in range(members):
+    for i in range(steps):
         fetch(i).start()
     limit = counts_ref[lax.axis_index("pw")]
-    row_slot = lax.broadcasted_iota(jnp.int32, (each * bands, length), 0) // bands
+    row_slot = lax.broadcasted_iota(jnp.int32, (GROUP * bands, length), 0) // bands
     table_copy.wait()
 
     def step(i, carry):
         fetch(i).wait()
-        turned = [
-            jnp.swapaxes(buf[i, :, s : s + GROUP, :], 0, 1).reshape(GROUP * bands, length)
-            for s in range(0, each, GROUP)
-        ]
-        value = dot(jnp.concatenate(turned, axis=0), table[...])
-        value = jnp.where(row_slot < limit - i * each, value, 0.0).astype(jnp.bfloat16)
-        out_ref[i] = value.reshape(each, bands, length)
+        for part in range(span // GROUP):
+            rows = slice(part * GROUP, (part + 1) * GROUP)
+            turned = jnp.swapaxes(buf[i, :, rows, :], 0, 1).reshape(GROUP * bands, length)
+            value = dot(turned, table[...])
+            value = jnp.where(row_slot < limit - (i * span + part * GROUP), value, 0.0)
+            value = value.astype(jnp.bfloat16).reshape(GROUP, bands, length)
+            member = i * (span // each) + part // per_member
+            first = part % per_member * GROUP
+            out_ref[member, first : first + GROUP] = value
         return carry
 
-    lax.fori_loop(0, members, step, 0)
+    lax.fori_loop(0, steps, step, 0)
 
 
 def transform(columns, counts, members):
     bands, slots, length = columns.shape
     each = slots // members
+    span = 2 * each
+    steps = slots // span
     return pl.pallas_call(
         transform_kernel,
         in_specs=[
@@ -71,9 +78,9 @@
         out_specs=pl.BlockSpec(memory_space=pltpu.VMEM),
         out_shape=jax.ShapeDtypeStruct((members, each, bands, length), jnp.bfloat16),
         scratch_shapes=[
-            pltpu.VMEM((members, bands, each, length), jnp.bfloat16),
+            pltpu.VMEM((steps, bands, span, length), jnp.bfloat16),
             pltpu.VMEM((length, length), jnp.bfloat16),
-            pltpu.SemaphoreType.DMA((members,)),
+            pltpu.SemaphoreType.DMA((steps,)),
             pltpu.SemaphoreType.DMA,
         ],
         compiler_params=params(44),
@@ -81,21 +88,12 @@
     )(counts, hartley(length), columns)
 
 
-def fetch_slots(sticks_ref, buf, sems, i, each):
-    rows = pl.ds(i * each, each)
-    return pltpu.make_async_copy(sticks_ref.at[:, rows], buf.at[:, rows], sems.at[i])
-
-
-def gram_kernel(each, sticks_ref, out_ref, buf, sems):
+def gram_kernel(each, sticks_ref, out_ref):
     members, slots, bands, length = sticks_ref.shape
     total = members * bands
-    steps = slots // each
-    for i in range(steps):
-        fetch_slots(sticks_ref, buf, sems, i, each).start()
     acc = jnp.zeros((total, total), jnp.float32)
-    for i in range(steps):
-        fetch_slots(sticks_ref, buf, sems, i, each).wait()
-        rows = [buf[:, i * each + s].reshape(total, length) for s in range(each)]
+    for i in range(0, slots, each):
+        rows = [sticks_ref[:, i + s].reshape(total, length) for s in range(each)]
         wide = jnp.concatenate(rows, axis=1)
         acc += lax.dot_general(
             wide, wide, (((1,), (1,)), ((), ())), preferred_element_type=jnp.float32
@@ -113,16 +111,28 @@
     total = members * bands
     return pl.pallas_call(
         functools.partial(gram_kernel, each),
-        in_specs=[pl.BlockSpec(memory_space=pltpu.HBM)],
+        in_specs=[pl.BlockSpec(memory_space=pltpu.VMEM)],
         out_specs=pl.BlockSpec(memory_space=pltpu.VMEM),
         out_shape=jax.ShapeDtypeStruct((total * total // 512, 4, 128), jnp.float32),
-        scratch_shapes=[
-            pltpu.VMEM(sticks.shape, jnp.bfloat16),
-            pltpu.SemaphoreType.DMA((slots // each,)),
-        ],
-        compiler_params=params(52),
+        compiler_params=params(20),
         name="gram",
     )(sticks)
+
+
+def spread_kernel(shares_ref, out_ref):
+    share = jnp.sum(shares_ref[...], axis=0, keepdims=True)
+    out_ref[...] = jnp.broadcast_to(share, out_ref.shape)
+
+
+def spread(shares):
+    return pl.pallas_call(
+        spread_kernel,
+        in_specs=[pl.BlockSpec(memory_space=pltpu.VMEM)],
+        out_specs=pl.BlockSpec(memory_space=pltpu.VMEM),
+        out_shape=jax.ShapeDtypeStruct(shares.shape, shares.dtype),
+        compiler_params=params(8),
+        name="spread",
+    )(shares)
 
 
 def split(value):
@@ -136,13 +146,9 @@
     return dot(left_high, right_high) + (dot(left_high, right_low) + dot(left_low, right_high))
 
 
-def rotate_kernel(each, counts_ref, sums_ref, sticks_ref, out_ref, buf, sems, turn_ref):
+def rotate_kernel(counts_ref, sums_ref, sticks_ref, out_ref, turn_ref):
     members, slots, bands, length = sticks_ref.shape
     size = members * bands
-    steps = slots // each
-    for i in range(steps):
-        fetch_slots(sticks_ref, buf, sems, i, each).start()
-
     live = counts_ref[0]
     for i in range(1, counts_ref.shape[0]):
         live += counts_ref[i]
@@ -169,32 +175,25 @@
     turn_ref[...] = (z_iter / jnp.sqrt(scale)).T.astype(jnp.bfloat16)
 
     turn = turn_ref[...]
-    for i in range(steps):
-        fetch_slots(sticks_ref, buf, sems, i, each).wait()
-    for i in range(steps):
-        for s in range(i * each, (i + 1) * each):
-            value = dot(turn, buf[:, s].reshape(size, length)).astype(jnp.bfloat16)
-            out_ref[:, s] = value.reshape(members, bands, length)
-
-
-def rotate(counts, sums, sticks, each):
+    for s in range(slots):
+        value = dot(turn, sticks_ref[:, s].reshape(size, length)).astype(jnp.bfloat16)
+        out_ref[:, s] = value.reshape(members, bands, length)
+
+
+def rotate(counts, sums, sticks):
     members, slots, bands, length = sticks.shape
     size = members * bands
     return pl.pallas_call(
-        functools.partial(rotate_kernel, each),
+        rotate_kernel,
         in_specs=[
             pl.BlockSpec(memory_space=pltpu.SMEM),
             pl.BlockSpec(memory_space=pltpu.VMEM),
-            pl.BlockSpec(memory_space=pltpu.HBM),
+            pl.BlockSpec(memory_space=pltpu.VMEM),
         ],
         out_specs=pl.BlockSpec(memory_space=pltpu.VMEM),
         out_shape=jax.ShapeDtypeStruct(sticks.shape, jnp.bfloat16),
-        scratch_shapes=[
-            pltpu.VMEM(sticks.shape, jnp.bfloat16),
-            pltpu.SemaphoreType.DMA((slots // each,)),
-            pltpu.VMEM((size, size), jnp.bfloat16),
-        ],
-        compiler_params=params(44),
+        scratch_shapes=[pltpu.VMEM((size, size), jnp.bfloat16)],
+        compiler_params=params(24),
         name="rotate",
     )(counts, sums, sticks)
 
@@ -236,19 +235,15 @@
     )(rotated)
 
 
-def whole_sum(shares, axes):
-    share = lax.all_to_all(shares, axes, 0, 0, tiled=True).sum(0)
-    spread = jnp.broadcast_to(share[None], shares.shape)
-    return lax.all_to_all(spread, axes, 0, 0, tiled=True)
-
-
 def make_local(members):
     def local(columns, counts):
-        send = transform(columns, counts, members)
-        sticks = lax.all_to_all(send, "band", 0, 0, tiled=True)
-        sums = whole_sum(gram(sticks, 8), ("band", "pw"))
-        rotated = rotate(counts, sums, sticks, 16)
-        return place(lax.all_to_all(rotated, "band", 0, 0, tiled=True))
+        def exchange(value, axes):
+            return lax.all_to_all(value, axes, 0, 0, tiled=True)
+
+        sticks = exchange(transform(columns, counts, members), "band")
+        shares = exchange(gram(sticks, 16), ("band", "pw"))
+        sums = exchange(spread(shares), ("band", "pw"))
+        return place(exchange(rotate(counts, sums, sticks), "band"))
 
     return local
 

time: 262 us -> 257 us (0.981)
  Pallas kernels: 25.3 us -> 20.7 us
    pallas_call x1, Pallas kernels: 6.64 us -> 2.35 us  [gram(): pl.pallas_call(functools.partial(gram_kernel, each), in_specs=[pl.BlockSp...]
    pallas_call x1 -> x2, Pallas kernels: 8.1 us -> 8.16 us  [the longest x1 7.99 us: rotate(): pl.pallas_call(rotate_kernel, in_specs=[pl.BlockSpec(memory_space=pltpu.S...]
where the time goes in v1:
time: 257 us
  blocking collectives  234 us (91%)
  Pallas kernels  20.7 us (8%)
    all_to_all x4, blocking collectives, exchange(): return lax.all_to_all(value, axes, 0, 0, tiled=True)  234 us
    pallas_call x1, Pallas kernels, rotate(): pl.pallas_call(rotate_kernel, in_specs=[pl.BlockSpec(memory_space=pltpu.S...  7.99 us
    pallas_call x1, Pallas kernels, transform(): pl.pallas_call(transform_kernel, in_specs=[pl.BlockSpec(memory_space=pltp...  6.69 us

profile of v1, /device:TPU:0, one launch (start us, length us, event | category | flops | bytes accessed | tf_op | source)
XLA Modules:
  0.0 256.7 jit_solution(10599069244737309507)
XLA Ops:
  0.0 0.0 copy-start
  0.0 0.9 copy-done
  0.9 0.0 copy-start.1
  0.9 0.7 copy-done.1
  1.6 6.7 %transform.1 = bf16[16,64,16,256]{3,2,1,0:T(8,128)(2,1)S(1)} custom-call(s32[8]{0:T(128)S(1)} %copy-done.1, bf16[256,256]{1,0:T(8,128)(2,1)S(1)} %copy-done, bf16[16,1024,256]{2,1,0:T(8,128)(2,1)} %columns_ref.1), custom_call_target="tpu_custom_call" | custom-call | tf_op jit(solution)/shard_map/transform/pallas_call | solution.py:71
  8.3 103.6 %all_to_all.20.sticks_ref = bf16[16,64,16,256]{3,2,1,0:T(8,128)(2,1)S(1)} all-to-all(bf16[16,64,16,256]{3,2,1,0:T(8,128)(2,1)S(1)} %transform.1), channel_id=1, replica_groups=mesh['band'=16,'pw'=8] {'band'}, dimensions={0} | all-to-all | bytes 16777216 | tf_op jit(solution)/shard_map/all_to_all | solution.py:241
  111.8 0.0 copy-start.2
  111.8 2.4 gram.1
  114.2 16.9 %all_to_all.21.shares_ref = f32[128,4,128]{2,1,0:T(4,128)S(1)} all-to-all(f32[128,4,128]{2,1,0:T(4,128)S(1)} %gram.1), channel_id=1, replica_groups=mesh['band'=16,'pw'=8] {'band','pw'}, dimensions={0} | all-to-all | bytes 524288 | tf_op jit(solution)/shard_map/all_to_all | solution.py:241
  131.0 0.2 spread.1
  131.2 15.2 %all_to_all.22.sums_ref = f32[128,4,128]{2,1,0:T(4,128)S(1)} all-to-all(f32[128,4,128]{2,1,0:T(4,128)S(1)} %spread.1), channel_id=1, replica_groups=mesh['band'=16,'pw'=8] {'band','pw'}, dimensions={0} | all-to-all | bytes 524288 | tf_op jit(solution)/shard_map/all_to_all | solution.py:241
  146.4 0.0 copy-done.2
  146.4 8.0 %rotate.1 = bf16[16,64,16,256]{3,2,1,0:T(8,128)(2,1)S(1)} custom-call(s32[8]{0:T(128)S(1)} %copy-done.2, f32[128,4,128]{2,1,0:T(4,128)S(1)} %all_to_all.22.sums_ref, bf16[16,64,16,256]{3,2,1,0:T(8,128)(2,1)S(1)} %all_to_all.20.sticks_ref), custom_call_target="tpu_custom_call" | custom-call | tf_op jit(solution)/shard_map/rotate/pallas_call | solution.py:186
  154.4 98.7 %all_to_all.23.in_ref = bf16[16,64,16,256]{3,2,1,0:T(8,128)(2,1)S(1)} all-to-all(bf16[16,64,16,256]{3,2,1,0:T(8,128)(2,1)S(1)} %rotate.1), channel_id=1, replica_groups=mesh['band'=16,'pw'=8] {'band'}, dimensions={0} | all-to-all | bytes 16777216 | tf_op jit(solution)/shard_map/all_to_all | solution.py:241
  253.2 3.5 %place.1 = bf16[16,1024,256]{2,1,0:T(8,128)(2,1)} custom-call(bf16[16,64,16,256]{3,2,1,0:T(8,128)(2,1)S(1)} %all_to_all.23.in_ref), custom_call_target="tpu_custom_call" | custom-call | tf_op jit(solution)/shard_map/place/pallas_call | solution.py:224
Async XLA Ops:
  0.0 0.9 copy-start
  0.9 0.7 copy-start.1
  111.8 34.6 %copy-start.2 = (s32[8]{0:T(128)S(1)}, s32[8]{0:T(128)}, u32[]{:S(2)}) copy-start(s32[8]{0:T(128)} %counts_ref.3) | copy-start | bytes 100

commit v2 on v1

--- a/solution.py
+++ b/solution.py
@@ -29,35 +29,60 @@
     return pltpu.CompilerParams(vmem_limit_bytes=mib * MIB)
 
 
-def transform_kernel(counts_ref, table_ref, columns_ref, out_ref, buf, table, sems, table_sem):
+def in_hbm(value):
+    return pltpu.with_memory_space_constraint(value, pltpu.HBM)
+
+
+def transform_kernel(counts_ref, table_ref, columns_ref, out_ref, buf, table, limits, *sems):
     members, each, bands, length = out_ref.shape
     steps = buf.shape[0]
     span = buf.shape[2]
     per_member = each // GROUP
+    read_sems, table_sem, counts_sem = sems
 
     def fetch(i):
         rows = pl.ds(pl.multiple_of(i * span, span), span)
-        return pltpu.make_async_copy(columns_ref.at[:, rows, :], buf.at[i], sems.at[i])
-
+        return pltpu.make_async_copy(columns_ref.at[:, rows, :], buf.at[i], read_sems.at[i])
+
+    counts_copy = pltpu.make_async_copy(counts_ref, limits, counts_sem)
     table_copy = pltpu.make_async_copy(table_ref, table, table_sem)
+    counts_copy.start()
     table_copy.start()
     for i in range(steps):
         fetch(i).start()
-    limit = counts_ref[lax.axis_index("pw")]
     row_slot = lax.broadcasted_iota(jnp.int32, (GROUP * bands, length), 0) // bands
+    counts_copy.wait()
     table_copy.wait()
+    limit = limits[lax.axis_index("pw")]
+
+    def groups(i):
+        for part in range(span // GROUP):
+            first = part % per_member * GROUP
+            member = i * (span // each) + part // per_member
+            yield part * GROUP, (member, slice(first, first + GROUP))
 
     def step(i, carry):
         fetch(i).wait()
-        for part in range(span // GROUP):
-            rows = slice(part * GROUP, (part + 1) * GROUP)
-            turned = jnp.swapaxes(buf[i, :, rows, :], 0, 1).reshape(GROUP * bands, length)
-            value = dot(turned, table[...])
-            value = jnp.where(row_slot < limit - (i * span + part * GROUP), value, 0.0)
-            value = value.astype(jnp.bfloat16).reshape(GROUP, bands, length)
-            member = i * (span // each) + part // per_member
-            first = part % per_member * GROUP
-            out_ref[member, first : first + GROUP] = value
+        left = limit - i * span
+
+        def value(start):
+            rows = buf[i, :, start : start + GROUP, :]
+            turned = jnp.swapaxes(rows, 0, 1).reshape(GROUP * bands, length)
+            return dot(turned, table[...])
+
+        def put(at, rows):
+            out_ref[at] = rows.astype(jnp.bfloat16).reshape(GROUP, bands, length)
+
+        @pl.when(left >= span)
+        def _():
+            for start, at in groups(i):
+                put(at, value(start))
+
+        @pl.when(left < span)
+        def _():
+            for start, at in groups(i):
+                put(at, jnp.where(row_slot < left - start, value(start), 0.0))
+
         return carry
 
     lax.fori_loop(0, steps, step, 0)
@@ -70,22 +95,20 @@
     steps = slots // span
     return pl.pallas_call(
         transform_kernel,
-        in_specs=[
-            pl.BlockSpec(memory_space=pltpu.SMEM),
-            pl.BlockSpec(memory_space=pltpu.HBM),
-            pl.BlockSpec(memory_space=pltpu.HBM),
-        ],
+        in_specs=[pl.BlockSpec(memory_space=pltpu.HBM)] * 3,
         out_specs=pl.BlockSpec(memory_space=pltpu.VMEM),
         out_shape=jax.ShapeDtypeStruct((members, each, bands, length), jnp.bfloat16),
         scratch_shapes=[
             pltpu.VMEM((steps, bands, span, length), jnp.bfloat16),
             pltpu.VMEM((length, length), jnp.bfloat16),
+            pltpu.SMEM(counts.shape, jnp.int32),
             pltpu.SemaphoreType.DMA((steps,)),
+            pltpu.SemaphoreType.DMA,
             pltpu.SemaphoreType.DMA,
         ],
         compiler_params=params(44),
         name="transform",
-    )(counts, hartley(length), columns)
+    )(in_hbm(counts), in_hbm(hartley(length)), in_hbm(columns))
 
 
 def gram_kernel(each, sticks_ref, out_ref):

time: 257 us -> 256 us (level)
  no operation moved by 1% of the time
where the time goes in v2:
time: 256 us
  blocking collectives  235 us (92%)
  Pallas kernels  21.2 us (8%)
    all_to_all x4, blocking collectives, exchange(): return lax.all_to_all(value, axes, 0, 0, tiled=True)  235 us
    pallas_call x1, Pallas kernels, rotate(): pl.pallas_call(rotate_kernel, in_specs=[pl.BlockSpec(memory_space=pltpu.S...  8 us
    pallas_call x1, Pallas kernels, transform(): pl.pallas_call(transform_kernel, in_specs=[pl.BlockSpec(memory_space=pltp...  7.07 us

profile of v2, /device:TPU:0, one launch (start us, length us, event | category | flops | bytes accessed | tf_op | source)
XLA Modules:
  0.0 255.9 jit_solution(14858111169238714572)
XLA Ops:
  0.0 7.1 %transform.1 = bf16[16,64,16,256]{3,2,1,0:T(8,128)(2,1)S(1)} custom-call(s32[8]{0:T(128)} %counts_ref.3, bf16[256,256]{1,0:T(8,128)(2,1)} %constant.2.clone.table_ref, bf16[16,1024,256]{2,1,0:T(8,128)(2,1)} %columns_ref.1), custom_call_target="tpu_custom_call" | custom-call | tf_op jit(solution)/shard_map/transform/pallas_call | solution.py:96
  7.1 103.6 %all_to_all.20.sticks_ref = bf16[16,64,16,256]{3,2,1,0:T(8,128)(2,1)S(1)} all-to-all(bf16[16,64,16,256]{3,2,1,0:T(8,128)(2,1)S(1)} %transform.1), channel_id=1, replica_groups=mesh['band'=16,'pw'=8] {'band'}, dimensions={0} | all-to-all | bytes 16777216 | tf_op jit(solution)/shard_map/all_to_all | solution.py:264
  110.6 0.0 copy-start
  110.6 2.5 gram.1
  113.1 17.2 %all_to_all.21.shares_ref = f32[128,4,128]{2,1,0:T(4,128)S(1)} all-to-all(f32[128,4,128]{2,1,0:T(4,128)S(1)} %gram.1), channel_id=1, replica_groups=mesh['band'=16,'pw'=8] {'band','pw'}, dimensions={0} | all-to-all | bytes 524288 | tf_op jit(solution)/shard_map/all_to_all | solution.py:264
  130.3 0.2 spread.1
  130.5 15.2 %all_to_all.22.sums_ref = f32[128,4,128]{2,1,0:T(4,128)S(1)} all-to-all(f32[128,4,128]{2,1,0:T(4,128)S(1)} %spread.1), channel_id=1, replica_groups=mesh['band'=16,'pw'=8] {'band','pw'}, dimensions={0} | all-to-all | bytes 524288 | tf_op jit(solution)/shard_map/all_to_all | solution.py:264
  145.7 0.0 copy-done
  145.7 8.0 %rotate.1 = bf16[16,64,16,256]{3,2,1,0:T(8,128)(2,1)S(1)} custom-call(s32[8]{0:T(128)S(1)} %copy-done, f32[128,4,128]{2,1,0:T(4,128)S(1)} %all_to_all.22.sums_ref, bf16[16,64,16,256]{3,2,1,0:T(8,128)(2,1)S(1)} %all_to_all.20.sticks_ref), custom_call_target="tpu_custom_call" | custom-call | tf_op jit(solution)/shard_map/rotate/pallas_call | solution.py:209
  153.7 98.7 %all_to_all.23.in_ref = bf16[16,64,16,256]{3,2,1,0:T(8,128)(2,1)S(1)} all-to-all(bf16[16,64,16,256]{3,2,1,0:T(8,128)(2,1)S(1)} %rotate.1), channel_id=1, replica_groups=mesh['band'=16,'pw'=8] {'band'}, dimensions={0} | all-to-all | bytes 16777216 | tf_op jit(solution)/shard_map/all_to_all | solution.py:264
  252.4 3.5 %place.1 = bf16[16,1024,256]{2,1,0:T(8,128)(2,1)} custom-call(bf16[16,64,16,256]{3,2,1,0:T(8,128)(2,1)S(1)} %all_to_all.23.in_ref), custom_call_target="tpu_custom_call" | custom-call | tf_op jit(solution)/shard_map/place/pallas_call | solution.py:247
Async XLA Ops:
  110.6 35.0 %copy-start = (s32[8]{0:T(128)S(1)}, s32[8]{0:T(128)}, u32[]{:S(2)}) copy-start(s32[8]{0:T(128)} %counts_ref.3) | copy-start | bytes 100

commit v3 on v2

--- a/solution.py
+++ b/solution.py
@@ -50,42 +50,44 @@
     table_copy.start()
     for i in range(steps):
         fetch(i).start()
-    row_slot = lax.broadcasted_iota(jnp.int32, (GROUP * bands, length), 0) // bands
     counts_copy.wait()
-    table_copy.wait()
     limit = limits[lax.axis_index("pw")]
-
-    def groups(i):
-        for part in range(span // GROUP):
-            first = part % per_member * GROUP
-            member = i * (span // each) + part // per_member
-            yield part * GROUP, (member, slice(first, first + GROUP))
+    live_steps = lax.div(limit + span - 1, span)
+    reached = live_steps * (span // GROUP)
 
     def step(i, carry):
         fetch(i).wait()
-        left = limit - i * span
-
-        def value(start):
+        for part in range(span // GROUP):
+            start = part * GROUP
             rows = buf[i, :, start : start + GROUP, :]
             turned = jnp.swapaxes(rows, 0, 1).reshape(GROUP * bands, length)
-            return dot(turned, table[...])
-
-        def put(at, rows):
-            out_ref[at] = rows.astype(jnp.bfloat16).reshape(GROUP, bands, length)
-
-        @pl.when(left >= span)
-        def _():
-            for start, at in groups(i):
-                put(at, value(start))
-
-        @pl.when(left < span)
-        def _():
-            for start, at in groups(i):
-                put(at, jnp.where(row_slot < left - start, value(start), 0.0))
-
-        return carry
-
-    lax.fori_loop(0, steps, step, 0)
+            value = dot(turned, table[...]).astype(jnp.bfloat16)
+            member = i * (span // each) + part // per_member
+            first = part % per_member * GROUP
+            out_ref[member, first : first + GROUP] = value.reshape(GROUP, bands, length)
+        return carry
+
+    def skip(i, carry):
+        fetch(i).wait()
+        return carry
+
+    def clear_group(g, carry):
+        first = pl.multiple_of(lax.rem(g, per_member) * GROUP, GROUP)
+        zeros = jnp.zeros((GROUP, bands, length), jnp.bfloat16)
+        out_ref[lax.div(g, per_member), pl.ds(first, GROUP)] = zeros
+        return carry
+
+    def clear_slot(s, carry):
+        out_ref[lax.div(s, each), lax.rem(s, each)] = jnp.zeros((bands, length), jnp.bfloat16)
+        return carry
+
+    lax.fori_loop(reached, members * per_member, clear_group, 0)
+    table_copy.wait()
+    lax.fori_loop(0, live_steps, step, 0)
+    whole = lax.div(limit + GROUP - 1, GROUP)
+    lax.fori_loop(limit, whole * GROUP, clear_slot, 0)
+    lax.fori_loop(whole, reached, clear_group, 0)
+    lax.fori_loop(live_steps, steps, skip, 0)
 
 
 def transform(columns, counts, members):
@@ -166,7 +168,9 @@
 def product(left, right):
     left_high, left_low = left
     right_high, right_low = right
-    return dot(left_high, right_high) + (dot(left_high, right_low) + dot(left_low, right_high))
+    both = dot(jnp.concatenate([left_high, left_low], axis=0), right_high)
+    rows = left_high.shape[0]
+    return both[:rows] + (both[rows:] + dot(left_high, right_low))
 
 
 def rotate_kernel(counts_ref, sums_ref, sticks_ref, out_ref, turn_ref):
@@ -186,15 +190,14 @@
     scale = jnp.sum(correlation * ident, keepdims=True) / size
     y_iter = correlation / scale
 
-    z_iter = 1.5 * ident - 0.5 * y_iter
-    z_split = split(z_iter)
-    y_split = split(product(split(y_iter), z_split))
+    t_iter = y_iter
+    z_iter = 1.5 * ident - 0.5 * t_iter
+    p_split = split(z_iter)
     for step in range(1, ITERS):
-        p_split = split(1.5 * ident - 0.5 * product(z_split, y_split))
-        if step < ITERS - 1:
-            y_split = split(product(y_split, p_split))
-        z_iter = product(p_split, z_split)
-        z_split = split(z_iter)
+        half = product(split(t_iter), p_split)
+        t_iter = product(split(half), p_split)
+        p_split = split(1.5 * ident - 0.5 * t_iter)
+        z_iter = product(p_split, split(z_iter))
     turn_ref[...] = (z_iter / jnp.sqrt(scale)).T.astype(jnp.bfloat16)
 
     turn = turn_ref[...]

time: 256 us -> 256 us (level)
  no operation moved by 1% of the time
where the time goes in v3:
time: 256 us
  blocking collectives  235 us (92%)
  Pallas kernels  20.6 us (8%)
    all_to_all x4, blocking collectives, exchange(): return lax.all_to_all(value, axes, 0, 0, tiled=True)  235 us
    pallas_call x1, Pallas kernels, rotate(): pl.pallas_call(rotate_kernel, in_specs=[pl.BlockSpec(memory_space=pltpu.S...  7.55 us
    pallas_call x1, Pallas kernels, transform(): pl.pallas_call(transform_kernel, in_specs=[pl.BlockSpec(memory_space=pltp...  7.02 us

profile of v3, /device:TPU:0, one launch (start us, length us, event | category | flops | bytes accessed | tf_op | source)
XLA Modules:
  0.0 255.5 jit_solution(11788581283133206166)
XLA Ops:
  0.0 7.0 %transform.1 = bf16[16,64,16,256]{3,2,1,0:T(8,128)(2,1)S(1)} custom-call(s32[8]{0:T(128)} %counts_ref.3, bf16[256,256]{1,0:T(8,128)(2,1)} %constant.2.clone.table_ref, bf16[16,1024,256]{2,1,0:T(8,128)(2,1)} %columns_ref.1), custom_call_target="tpu_custom_call" | custom-call | tf_op jit(solution)/shard_map/transform/pallas_call | solution.py:98
  7.0 103.6 %all_to_all.20.sticks_ref = bf16[16,64,16,256]{3,2,1,0:T(8,128)(2,1)S(1)} all-to-all(bf16[16,64,16,256]{3,2,1,0:T(8,128)(2,1)S(1)} %transform.1), channel_id=1, replica_groups=mesh['band'=16,'pw'=8] {'band'}, dimensions={0} | all-to-all | bytes 16777216 | tf_op jit(solution)/shard_map/all_to_all | solution.py:267
  110.6 0.0 copy-start
  110.6 2.4 gram.1
  113.0 17.4 %all_to_all.21.shares_ref = f32[128,4,128]{2,1,0:T(4,128)S(1)} all-to-all(f32[128,4,128]{2,1,0:T(4,128)S(1)} %gram.1), channel_id=1, replica_groups=mesh['band'=16,'pw'=8] {'band','pw'}, dimensions={0} | all-to-all | bytes 524288 | tf_op jit(solution)/shard_map/all_to_all | solution.py:267
  130.3 0.2 spread.1
  130.5 15.2 %all_to_all.22.sums_ref = f32[128,4,128]{2,1,0:T(4,128)S(1)} all-to-all(f32[128,4,128]{2,1,0:T(4,128)S(1)} %spread.1), channel_id=1, replica_groups=mesh['band'=16,'pw'=8] {'band','pw'}, dimensions={0} | all-to-all | bytes 524288 | tf_op jit(solution)/shard_map/all_to_all | solution.py:267
  145.7 0.0 copy-done
  145.7 7.6 %rotate.1 = bf16[16,64,16,256]{3,2,1,0:T(8,128)(2,1)S(1)} custom-call(s32[8]{0:T(128)S(1)} %copy-done, f32[128,4,128]{2,1,0:T(4,128)S(1)} %all_to_all.22.sums_ref, bf16[16,64,16,256]{3,2,1,0:T(8,128)(2,1)S(1)} %all_to_all.20.sticks_ref), custom_call_target="tpu_custom_call" | custom-call | tf_op jit(solution)/shard_map/rotate/pallas_call | solution.py:212
  153.2 98.7 %all_to_all.23.in_ref = bf16[16,64,16,256]{3,2,1,0:T(8,128)(2,1)S(1)} all-to-all(bf16[16,64,16,256]{3,2,1,0:T(8,128)(2,1)S(1)} %rotate.1), channel_id=1, replica_groups=mesh['band'=16,'pw'=8] {'band'}, dimensions={0} | all-to-all | bytes 16777216 | tf_op jit(solution)/shard_map/all_to_all | solution.py:267
  252.0 3.5 %place.1 = bf16[16,1024,256]{2,1,0:T(8,128)(2,1)} custom-call(bf16[16,64,16,256]{3,2,1,0:T(8,128)(2,1)S(1)} %all_to_all.23.in_ref), custom_call_target="tpu_custom_call" | custom-call | tf_op jit(solution)/shard_map/place/pallas_call | solution.py:250
Async XLA Ops:
  110.6 35.1 %copy-start = (s32[8]{0:T(128)S(1)}, s32[8]{0:T(128)}, u32[]{:S(2)}) copy-start(s32[8]{0:T(128)} %counts_ref.3) | copy-start | bytes 100

commit v4 on v3

--- a/solution.py
+++ b/solution.py
@@ -93,7 +93,7 @@
 def transform(columns, counts, members):
     bands, slots, length = columns.shape
     each = slots // members
-    span = 2 * each
+    span = 4 * each
     steps = slots // span
     return pl.pallas_call(
         transform_kernel,
@@ -198,7 +198,7 @@
         t_iter = product(split(half), p_split)
         p_split = split(1.5 * ident - 0.5 * t_iter)
         z_iter = product(p_split, split(z_iter))
-    turn_ref[...] = (z_iter / jnp.sqrt(scale)).T.astype(jnp.bfloat16)
+    turn_ref[...] = (z_iter / jnp.sqrt(scale)).astype(jnp.bfloat16)
 
     turn = turn_ref[...]
     for s in range(slots):
@@ -267,7 +267,7 @@
             return lax.all_to_all(value, axes, 0, 0, tiled=True)
 
         sticks = exchange(transform(columns, counts, members), "band")
-        shares = exchange(gram(sticks, 16), ("band", "pw"))
+        shares = exchange(gram(sticks, 32), ("band", "pw"))
         sums = exchange(spread(shares), ("band", "pw"))
         return place(exchange(rotate(counts, sums, sticks), "band"))
 

time: 256 us -> 256 us (level)
  no operation moved by 1% of the time
where the time goes in v4:
time: 256 us; the launch traced here: 255 us
  blocking collectives  237 us (93%)
  Pallas kernels  18.1 us (7%)
    all_to_all x4, blocking collectives, exchange(): return lax.all_to_all(value, axes, 0, 0, tiled=True)  237 us
    pallas_call x1, Pallas kernels, rotate(): pl.pallas_call(rotate_kernel, in_specs=[pl.BlockSpec(memory_space=pltpu.S...  7.46 us

profile of v4, /device:TPU:0, one launch (start us, length us, event | category | flops | bytes accessed | tf_op | source)
XLA Modules:
  0.0 255.2 jit_solution(9770457573645474538)
XLA Ops:
  0.0 4.6 %transform.1 = bf16[16,64,16,256]{3,2,1,0:T(8,128)(2,1)S(1)} custom-call(s32[8]{0:T(128)} %counts_ref.3, bf16[256,256]{1,0:T(8,128)(2,1)} %constant.2.clone.table_ref, bf16[16,1024,256]{2,1,0:T(8,128)(2,1)} %columns_ref.1), custom_call_target="tpu_custom_call" | custom-call | tf_op jit(solution)/shard_map/transform/pallas_call | solution.py:98
  4.6 105.0 %all_to_all.20.sticks_ref = bf16[16,64,16,256]{3,2,1,0:T(8,128)(2,1)S(1)} all-to-all(bf16[16,64,16,256]{3,2,1,0:T(8,128)(2,1)S(1)} %transform.1), channel_id=1, replica_groups=mesh['band'=16,'pw'=8] {'band'}, dimensions={0} | all-to-all | bytes 16777216 | tf_op jit(solution)/shard_map/all_to_all | solution.py:267
  109.6 0.0 copy-start
  109.6 2.4 gram.1
  112.0 18.2 %all_to_all.21.shares_ref = f32[128,4,128]{2,1,0:T(4,128)S(1)} all-to-all(f32[128,4,128]{2,1,0:T(4,128)S(1)} %gram.1), channel_id=1, replica_groups=mesh['band'=16,'pw'=8] {'band','pw'}, dimensions={0} | all-to-all | bytes 524288 | tf_op jit(solution)/shard_map/all_to_all | solution.py:267
  130.1 0.2 spread.1
  130.3 15.2 %all_to_all.22.sums_ref = f32[128,4,128]{2,1,0:T(4,128)S(1)} all-to-all(f32[128,4,128]{2,1,0:T(4,128)S(1)} %spread.1), channel_id=1, replica_groups=mesh['band'=16,'pw'=8] {'band','pw'}, dimensions={0} | all-to-all | bytes 524288 | tf_op jit(solution)/shard_map/all_to_all | solution.py:267
  145.5 0.0 copy-done
  145.5 7.5 %rotate.1 = bf16[16,64,16,256]{3,2,1,0:T(8,128)(2,1)S(1)} custom-call(s32[8]{0:T(128)S(1)} %copy-done, f32[128,4,128]{2,1,0:T(4,128)S(1)} %all_to_all.22.sums_ref, bf16[16,64,16,256]{3,2,1,0:T(8,128)(2,1)S(1)} %all_to_all.20.sticks_ref), custom_call_target="tpu_custom_call" | custom-call | tf_op jit(solution)/shard_map/rotate/pallas_call | solution.py:212
  153.0 98.7 %all_to_all.23.in_ref = bf16[16,64,16,256]{3,2,1,0:T(8,128)(2,1)S(1)} all-to-all(bf16[16,64,16,256]{3,2,1,0:T(8,128)(2,1)S(1)} %rotate.1), channel_id=1, replica_groups=mesh['band'=16,'pw'=8] {'band'}, dimensions={0} | all-to-all | bytes 16777216 | tf_op jit(solution)/shard_map/all_to_all | solution.py:267
  251.7 3.5 %place.1 = bf16[16,1024,256]{2,1,0:T(8,128)(2,1)} custom-call(bf16[16,64,16,256]{3,2,1,0:T(8,128)(2,1)S(1)} %all_to_all.23.in_ref), custom_call_target="tpu_custom_call" | custom-call | tf_op jit(solution)/shard_map/place/pallas_call | solution.py:250
Async XLA Ops:
  109.6 35.9 %copy-start = (s32[8]{0:T(128)S(1)}, s32[8]{0:T(128)}, u32[]{:S(2)}) copy-start(s32[8]{0:T(128)} %counts_ref.3) | copy-start | bytes 100

commit v5 on v4

--- a/solution.py
+++ b/solution.py
@@ -33,43 +33,35 @@
     return pltpu.with_memory_space_constraint(value, pltpu.HBM)
 
 
+def slot_chunks(slots):
+    marks = [0, slots // 16, 3 * slots // 16, 7 * slots // 16, 11 * slots // 16, slots]
+    marks = sorted({mark - mark % GROUP for mark in marks})
+    return list(zip(marks[:-1], marks[1:]))
+
+
 def transform_kernel(counts_ref, table_ref, columns_ref, out_ref, buf, table, limits, *sems):
     members, each, bands, length = out_ref.shape
-    steps = buf.shape[0]
-    span = buf.shape[2]
+    slots = buf.shape[1]
     per_member = each // GROUP
     read_sems, table_sem, counts_sem = sems
+    chunks = slot_chunks(slots)
 
     def fetch(i):
-        rows = pl.ds(pl.multiple_of(i * span, span), span)
-        return pltpu.make_async_copy(columns_ref.at[:, rows, :], buf.at[i], read_sems.at[i])
+        first, last = chunks[i]
+        rows = pl.ds(first, last - first)
+        return pltpu.make_async_copy(columns_ref.at[:, rows, :], buf.at[:, rows, :], read_sems.at[i])
 
     counts_copy = pltpu.make_async_copy(counts_ref, limits, counts_sem)
     table_copy = pltpu.make_async_copy(table_ref, table, table_sem)
     counts_copy.start()
     table_copy.start()
-    for i in range(steps):
+    for i in range(len(chunks)):
         fetch(i).start()
     counts_copy.wait()
     limit = limits[lax.axis_index("pw")]
-    live_steps = lax.div(limit + span - 1, span)
-    reached = live_steps * (span // GROUP)
-
-    def step(i, carry):
-        fetch(i).wait()
-        for part in range(span // GROUP):
-            start = part * GROUP
-            rows = buf[i, :, start : start + GROUP, :]
-            turned = jnp.swapaxes(rows, 0, 1).reshape(GROUP * bands, length)
-            value = dot(turned, table[...]).astype(jnp.bfloat16)
-            member = i * (span // each) + part // per_member
-            first = part % per_member * GROUP
-            out_ref[member, first : first + GROUP] = value.reshape(GROUP, bands, length)
-        return carry
-
-    def skip(i, carry):
-        fetch(i).wait()
-        return carry
+    reached = 0
+    for first, last in chunks:
+        reached = jnp.where(limit > first, last // GROUP, reached)
 
     def clear_group(g, carry):
         first = pl.multiple_of(lax.rem(g, per_member) * GROUP, GROUP)
@@ -83,25 +75,34 @@
 
     lax.fori_loop(reached, members * per_member, clear_group, 0)
     table_copy.wait()
-    lax.fori_loop(0, live_steps, step, 0)
+    for i, (begin, end) in enumerate(chunks):
+        fetch(i).wait()
+
+        @pl.when(limit > begin)
+        def _():
+            for start in range(begin, end, GROUP):
+                rows = buf[:, start : start + GROUP, :]
+                turned = jnp.swapaxes(rows, 0, 1).reshape(GROUP * bands, length)
+                value = dot(turned, table[...]).astype(jnp.bfloat16)
+                first = start % each
+                out_ref[start // each, first : first + GROUP] = value.reshape(GROUP, bands, length)
+
     whole = lax.div(limit + GROUP - 1, GROUP)
     lax.fori_loop(limit, whole * GROUP, clear_slot, 0)
     lax.fori_loop(whole, reached, clear_group, 0)
-    lax.fori_loop(live_steps, steps, skip, 0)
 
 
 def transform(columns, counts, members):
     bands, slots, length = columns.shape
     each = slots // members
-    span = 4 * each
-    steps = slots // span
+    steps = len(slot_chunks(slots))
     return pl.pallas_call(
         transform_kernel,
         in_specs=[pl.BlockSpec(memory_space=pltpu.HBM)] * 3,
         out_specs=pl.BlockSpec(memory_space=pltpu.VMEM),
         out_shape=jax.ShapeDtypeStruct((members, each, bands, length), jnp.bfloat16),
         scratch_shapes=[
-            pltpu.VMEM((steps, bands, span, length), jnp.bfloat16),
+            pltpu.VMEM((bands, slots, length), jnp.bfloat16),
             pltpu.VMEM((length, length), jnp.bfloat16),
             pltpu.SMEM(counts.shape, jnp.int32),
             pltpu.SemaphoreType.DMA((steps,)),

time: 256 us -> 254 us (level)
  no operation moved by 1% of the time
where the time goes in v5:
time: 254 us
  blocking collectives  235 us (93%)
  Pallas kernels  18.7 us (7%)
    all_to_all x4, blocking collectives, exchange(): return lax.all_to_all(value, axes, 0, 0, tiled=True)  235 us
    pallas_call x1, Pallas kernels, rotate(): pl.pallas_call(rotate_kernel, in_specs=[pl.BlockSpec(memory_space=pltpu.S...  7.45 us
    pallas_call x1, Pallas kernels, transform(): pl.pallas_call(transform_kernel, in_specs=[pl.BlockSpec(memory_space=pltp...  5.16 us

profile of v5, /device:TPU:0, one launch (start us, length us, event | category | flops | bytes accessed | tf_op | source)
XLA Modules:
  0.0 254.0 jit_solution(5737443788072107127)
XLA Ops:
  0.0 5.2 %transform.1 = bf16[16,64,16,256]{3,2,1,0:T(8,128)(2,1)S(1)} custom-call(s32[8]{0:T(128)} %counts_ref.3, bf16[256,256]{1,0:T(8,128)(2,1)} %constant.2.clone.table_ref, bf16[16,1024,256]{2,1,0:T(8,128)(2,1)} %columns_ref.1), custom_call_target="tpu_custom_call" | custom-call | tf_op jit(solution)/shard_map/transform/pallas_call | solution.py:99
  5.2 103.5 %all_to_all.20.sticks_ref = bf16[16,64,16,256]{3,2,1,0:T(8,128)(2,1)S(1)} all-to-all(bf16[16,64,16,256]{3,2,1,0:T(8,128)(2,1)S(1)} %transform.1), channel_id=1, replica_groups=mesh['band'=16,'pw'=8] {'band'}, dimensions={0} | all-to-all | bytes 16777216 | tf_op jit(solution)/shard_map/all_to_all | solution.py:268
  108.7 0.0 copy-start
  108.7 2.4 gram.1
  111.0 17.8 %all_to_all.21.shares_ref = f32[128,4,128]{2,1,0:T(4,128)S(1)} all-to-all(f32[128,4,128]{2,1,0:T(4,128)S(1)} %gram.1), channel_id=1, replica_groups=mesh['band'=16,'pw'=8] {'band','pw'}, dimensions={0} | all-to-all | bytes 524288 | tf_op jit(solution)/shard_map/all_to_all | solution.py:268
  128.9 0.2 spread.1
  129.0 15.2 %all_to_all.22.sums_ref = f32[128,4,128]{2,1,0:T(4,128)S(1)} all-to-all(f32[128,4,128]{2,1,0:T(4,128)S(1)} %spread.1), channel_id=1, replica_groups=mesh['band'=16,'pw'=8] {'band','pw'}, dimensions={0} | all-to-all | bytes 524288 | tf_op jit(solution)/shard_map/all_to_all | solution.py:268
  144.2 0.0 copy-done
  144.2 7.5 %rotate.1 = bf16[16,64,16,256]{3,2,1,0:T(8,128)(2,1)S(1)} custom-call(s32[8]{0:T(128)S(1)} %copy-done, f32[128,4,128]{2,1,0:T(4,128)S(1)} %all_to_all.22.sums_ref, bf16[16,64,16,256]{3,2,1,0:T(8,128)(2,1)S(1)} %all_to_all.20.sticks_ref), custom_call_target="tpu_custom_call" | custom-call | tf_op jit(solution)/shard_map/rotate/pallas_call | solution.py:213
  151.7 98.7 %all_to_all.23.in_ref = bf16[16,64,16,256]{3,2,1,0:T(8,128)(2,1)S(1)} all-to-all(bf16[16,64,16,256]{3,2,1,0:T(8,128)(2,1)S(1)} %rotate.1), channel_id=1, replica_groups=mesh['band'=16,'pw'=8] {'band'}, dimensions={0} | all-to-all | bytes 16777216 | tf_op jit(solution)/shard_map/all_to_all | solution.py:268
  250.5 3.5 %place.1 = bf16[16,1024,256]{2,1,0:T(8,128)(2,1)} custom-call(bf16[16,64,16,256]{3,2,1,0:T(8,128)(2,1)S(1)} %all_to_all.23.in_ref), custom_call_target="tpu_custom_call" | custom-call | tf_op jit(solution)/shard_map/place/pallas_call | solution.py:251
Async XLA Ops:
  108.7 35.6 %copy-start = (s32[8]{0:T(128)S(1)}, s32[8]{0:T(128)}, u32[]{:S(2)}) copy-start(s32[8]{0:T(128)} %counts_ref.3) | copy-start | bytes 100

commit v6 on v5

--- a/solution.py
+++ b/solution.py
@@ -34,7 +34,7 @@
 
 
 def slot_chunks(slots):
-    marks = [0, slots // 16, 3 * slots // 16, 7 * slots // 16, 11 * slots // 16, slots]
+    marks = [part * slots // 16 for part in (0, 1, 3, 6, 9, 12, 16)]
     marks = sorted({mark - mark % GROUP for mark in marks})
     return list(zip(marks[:-1], marks[1:]))
 
@@ -57,35 +57,36 @@
     table_copy.start()
     for i in range(len(chunks)):
         fetch(i).start()
+    def clear_group(g, carry):
+        first = pl.multiple_of(lax.rem(g, per_member) * GROUP, GROUP)
+        zeros = jnp.zeros((GROUP, bands, length), jnp.bfloat16)
+        out_ref[lax.div(g, per_member), pl.ds(first, GROUP)] = zeros
+        return carry
+
+    def clear_slot(s, carry):
+        out_ref[lax.div(s, each), lax.rem(s, each)] = jnp.zeros((bands, length), jnp.bfloat16)
+        return carry
+
+    def work(begin, end):
+        for start in range(begin, end, GROUP):
+            rows = buf[:, start : start + GROUP, :]
+            turned = jnp.swapaxes(rows, 0, 1).reshape(GROUP * bands, length)
+            value = dot(turned, table[...]).astype(jnp.bfloat16)
+            first = start % each
+            out_ref[start // each, first : first + GROUP] = value.reshape(GROUP, bands, length)
+
+    table_copy.wait()
+    fetch(0).wait()
+    work(*chunks[0])
     counts_copy.wait()
     limit = limits[lax.axis_index("pw")]
     reached = 0
     for first, last in chunks:
         reached = jnp.where(limit > first, last // GROUP, reached)
-
-    def clear_group(g, carry):
-        first = pl.multiple_of(lax.rem(g, per_member) * GROUP, GROUP)
-        zeros = jnp.zeros((GROUP, bands, length), jnp.bfloat16)
-        out_ref[lax.div(g, per_member), pl.ds(first, GROUP)] = zeros
-        return carry
-
-    def clear_slot(s, carry):
-        out_ref[lax.div(s, each), lax.rem(s, each)] = jnp.zeros((bands, length), jnp.bfloat16)
-        return carry
-
     lax.fori_loop(reached, members * per_member, clear_group, 0)
-    table_copy.wait()
-    for i, (begin, end) in enumerate(chunks):
+    for i in range(1, len(chunks)):
         fetch(i).wait()
-
-        @pl.when(limit > begin)
-        def _():
-            for start in range(begin, end, GROUP):
-                rows = buf[:, start : start + GROUP, :]
-                turned = jnp.swapaxes(rows, 0, 1).reshape(GROUP * bands, length)
-                value = dot(turned, table[...]).astype(jnp.bfloat16)
-                first = start % each
-                out_ref[start // each, first : first + GROUP] = value.reshape(GROUP, bands, length)
+        pl.when(limit > chunks[i][0])(functools.partial(work, *chunks[i]))
 
     whole = lax.div(limit + GROUP - 1, GROUP)
     lax.fori_loop(limit, whole * GROUP, clear_slot, 0)

time: 254 us -> 254 us (level)
  no operation moved by 1% of the time
where the time goes in v6:
time: 254 us
  blocking collectives  234 us (92%)
  Pallas kernels  20.1 us (8%)
    all_to_all x4, blocking collectives, exchange(): return lax.all_to_all(value, axes, 0, 0, tiled=True)  234 us
    pallas_call x1, Pallas kernels, rotate(): pl.pallas_call(rotate_kernel, in_specs=[pl.BlockSpec(memory_space=pltpu.S...  7.45 us
    pallas_call x1, Pallas kernels, transform(): pl.pallas_call(transform_kernel, in_specs=[pl.BlockSpec(memory_space=pltp...  6.6 us

profile of v6, /device:TPU:0, one launch (start us, length us, event | category | flops | bytes accessed | tf_op | source)
XLA Modules:
  0.0 254.2 jit_solution(15459953586294029330)
XLA Ops:
  0.0 6.6 %transform.1 = bf16[16,64,16,256]{3,2,1,0:T(8,128)(2,1)S(1)} custom-call(s32[8]{0:T(128)} %counts_ref.3, bf16[256,256]{1,0:T(8,128)(2,1)} %constant.2.clone.table_ref, bf16[16,1024,256]{2,1,0:T(8,128)(2,1)} %columns_ref.1), custom_call_target="tpu_custom_call" | custom-call | tf_op jit(solution)/shard_map/transform/pallas_call | solution.py:100
  6.6 103.4 %all_to_all.20.sticks_ref = bf16[16,64,16,256]{3,2,1,0:T(8,128)(2,1)S(1)} all-to-all(bf16[16,64,16,256]{3,2,1,0:T(8,128)(2,1)S(1)} %transform.1), channel_id=1, replica_groups=mesh['band'=16,'pw'=8] {'band'}, dimensions={0} | all-to-all | bytes 16777216 | tf_op jit(solution)/shard_map/all_to_all | solution.py:269
  110.0 0.0 copy-start
  110.0 2.4 gram.1
  112.3 16.7 %all_to_all.21.shares_ref = f32[128,4,128]{2,1,0:T(4,128)S(1)} all-to-all(f32[128,4,128]{2,1,0:T(4,128)S(1)} %gram.1), channel_id=1, replica_groups=mesh['band'=16,'pw'=8] {'band','pw'}, dimensions={0} | all-to-all | bytes 524288 | tf_op jit(solution)/shard_map/all_to_all | solution.py:269
  129.0 0.2 spread.1
  129.2 15.2 %all_to_all.22.sums_ref = f32[128,4,128]{2,1,0:T(4,128)S(1)} all-to-all(f32[128,4,128]{2,1,0:T(4,128)S(1)} %spread.1), channel_id=1, replica_groups=mesh['band'=16,'pw'=8] {'band','pw'}, dimensions={0} | all-to-all | bytes 524288 | tf_op jit(solution)/shard_map/all_to_all | solution.py:269
  144.4 0.0 copy-done
  144.4 7.5 %rotate.1 = bf16[16,64,16,256]{3,2,1,0:T(8,128)(2,1)S(1)} custom-call(s32[8]{0:T(128)S(1)} %copy-done, f32[128,4,128]{2,1,0:T(4,128)S(1)} %all_to_all.22.sums_ref, bf16[16,64,16,256]{3,2,1,0:T(8,128)(2,1)S(1)} %all_to_all.20.sticks_ref), custom_call_target="tpu_custom_call" | custom-call | tf_op jit(solution)/shard_map/rotate/pallas_call | solution.py:214
  151.9 98.7 %all_to_all.23.in_ref = bf16[16,64,16,256]{3,2,1,0:T(8,128)(2,1)S(1)} all-to-all(bf16[16,64,16,256]{3,2,1,0:T(8,128)(2,1)S(1)} %rotate.1), channel_id=1, replica_groups=mesh['band'=16,'pw'=8] {'band'}, dimensions={0} | all-to-all | bytes 16777216 | tf_op jit(solution)/shard_map/all_to_all | solution.py:269
  250.6 3.5 %place.1 = bf16[16,1024,256]{2,1,0:T(8,128)(2,1)} custom-call(bf16[16,64,16,256]{3,2,1,0:T(8,128)(2,1)S(1)} %all_to_all.23.in_ref), custom_call_target="tpu_custom_call" | custom-call | tf_op jit(solution)/shard_map/place/pallas_call | solution.py:252
Async XLA Ops:
  110.0 34.4 %copy-start = (s32[8]{0:T(128)S(1)}, s32[8]{0:T(128)}, u32[]{:S(2)}) copy-start(s32[8]{0:T(128)} %counts_ref.3) | copy-start | bytes 100
